TPU v7x, 256 devices: a whole 4x4x8 slice. The times are simulated.
256 devices in a mesh: sub: 64 (over z, x, core), crs: 4 (over y).
Axes of the slice: x: 4, y: 4, z: 8, core: 2. Of those that a mesh axis runs over, the one named last changes fastest.
Arguments:
- right_sides: bfloat16 [64, 2304, 512], P('sub'), may hold values from -40 to 40
- stiffness_shift: float32 [64, 2304], P('sub'), may hold values from 0.5 to 8
- local_inverses: bfloat16 [64, 2304, 2304], P('sub', 'crs'), may hold values from -0.5 to 0.5
- eigen_basis: bfloat16 [64, 32, 2304], P('sub'), may hold values from -0.125 to 0.125
- eigen_counts: int32 [64], P('sub'), may hold values from 16 to 32, as said below
- face_indices: int32 [64, 2, 576], P('sub'), may hold values from 0 to 2303, as said below
- coarse_inverse: bfloat16 [2048, 2048], P('crs'), may hold values from -2 to 2
Outputs:
- solution: bfloat16 [64, 2304, 512], P('sub')
- residual_estimate: float32 [512], replicated
Inputs may be any that keep to these rules, and one draw needn't show every extreme that they name: `eigen_counts`: some subdomain keeps 32. `face_indices`: the 1152 indices of one subdomain are distinct.
All inputs are finite; a program needn't handle non-finite values.
Results may differ from a plain program's by a relative error of at most 0.006.
Values may be sent and summed in bfloat16 or wider, within the bound.
A program may use at most 128 MiB of HBM per device.

v0:
```python
import jax
import jax.numpy as jnp
from jax import lax
from jax.sharding import PartitionSpec as P


def padded_2(block, sides, width):
    for axis, dim in sides:
        count = lax.axis_size(axis)
        forward = [(i, i + 1) for i in range(count - 1)]
        backward = [(target, source) for source, target in forward]
        low = lax.ppermute(
            lax.slice_in_dim(block, block.shape[dim] - width, None, axis=dim), axis, forward
        )
        high = lax.ppermute(lax.slice_in_dim(block, 0, width, axis=dim), axis, backward)
        block = jnp.concatenate([low, block, high], axis=dim)
    return block


def broadcast(block, axis, owner):
    block = jnp.where(lax.axis_index(axis) == owner, block, jnp.zeros_like(block))
    return lax.psum(block, axis)


def neighbour_rims(vector_in, face_rows):
    face_length = face_rows.shape[1]
    width_rhs = vector_in.shape[1]
    rim_values = jnp.take(vector_in, face_rows.reshape(-1), axis=0).reshape(
        2, face_length, width_rhs
    )
    padded = padded_2(rim_values, (("sub", 0),), 1)
    from_below = padded[0]
    from_above = padded[3]
    return (from_below, from_above)


def apply_operator(vector_in, shift_grid, face_rows):
    dof_count, width_rhs = vector_in.shape
    from_below, from_above = neighbour_rims(vector_in, face_rows)
    component_grid = vector_in.reshape(3, dof_count // 3, width_rhs)
    zero_column = jnp.zeros((3, 1, width_rhs), jnp.float32)
    below_cells = jnp.concatenate([zero_column, component_grid[:, :-1]], axis=1)
    above_cells = jnp.concatenate([component_grid[:, 1:], zero_column], axis=1)
    cross_terms = jnp.sum(component_grid, axis=0, keepdims=True) - component_grid
    applied = (6.0 + shift_grid) * component_grid - below_cells - above_cells - 0.5 * cross_terms
    applied = applied.reshape(dof_count, width_rhs)
    applied = applied.at[face_rows[0]].add(-4.0 * from_below)
    return applied.at[face_rows[1]].add(-4.0 * from_above)


def inner_sum(first_vec, second_vec):
    return lax.psum(jnp.sum(first_vec * second_vec, axis=0), "sub")


def norm_of(vector_in):
    return jnp.sqrt(lax.psum(jnp.sum(vector_in * vector_in, axis=0), "sub") + 1e-12)


def per_device(
    right_sides,
    stiffness_shift,
    local_inverses,
    eigen_basis,
    eigen_counts,
    face_indices,
    coarse_inverse,
):
    sub_index = lax.axis_index("sub")
    sub_count = lax.axis_size("sub")
    crs_count = lax.axis_size("crs")
    source = right_sides[0].astype(jnp.float32)
    dof_count, width_rhs = source.shape
    shift_grid = stiffness_shift[0].reshape(3, dof_count // 3, 1)
    face_rows = face_indices[0]
    inverse_rows = local_inverses[0]
    basis_width = eigen_basis.shape[1]
    column_index = lax.broadcasted_iota(jnp.int32, (basis_width, 1), 0)
    masked_basis = jnp.where(
        column_index < eigen_counts[0], eigen_basis[0], jnp.zeros_like(eigen_basis[0])
    )
    panel_rows = coarse_inverse.shape[0]
    offset_rows = sub_index * basis_width % panel_rows
    owner_index = sub_index // (sub_count // crs_count)

    def precondition(vector_in):
        vector_half = vector_in.astype(jnp.bfloat16)
        local_part = jnp.dot(inverse_rows, vector_half, preferred_element_type=jnp.float32).astype(
            jnp.bfloat16
        )
        local_whole = lax.all_gather(local_part, "crs", axis=0, tiled=True)
        coefficients = jnp.dot(
            masked_basis, vector_half, preferred_element_type=jnp.float32
        ).astype(jnp.bfloat16)
        own_rows = lax.dynamic_slice_in_dim(coarse_inverse, offset_rows, basis_width, 0)
        own_coarse = jnp.dot(
            own_rows,
            lax.all_gather(coefficients, "sub", axis=0, tiled=True),
            preferred_element_type=jnp.float32,
        )
        coarse_values = broadcast(own_coarse.astype(jnp.bfloat16), "crs", owner_index)
        correction = lax.dot_general(
            masked_basis,
            coarse_values,
            (((0,), (0,)), ((), ())),
            preferred_element_type=jnp.float32,
        )
        return (local_whole.astype(jnp.float32) + correction, local_whole, coarse_values)

    beta = norm_of(source)
    first = source / beta
    z_one, local_one, coarse_one = precondition(first)
    w_one = apply_operator(z_one, shift_grid, face_rows)
    h11 = inner_sum(w_one, first)
    w_one = w_one - h11 * first
    h21 = norm_of(w_one)
    second = w_one / h21
    z_two, local_two, coarse_two = precondition(second)
    w_two = apply_operator(z_two, shift_grid, face_rows)
    h12 = inner_sum(w_two, first)
    w_two = w_two - h12 * first
    h22 = inner_sum(w_two, second)
    w_two = w_two - h22 * second
    h32 = norm_of(w_two)
    dist_one = jnp.sqrt(h11 * h11 + h21 * h21)
    cos_one = h11 / dist_one
    sin_one = h21 / dist_one
    r12 = cos_one * h12 + sin_one * h22
    t22 = cos_one * h22 - sin_one * h12
    dist_two = jnp.sqrt(t22 * t22 + h32 * h32)
    cos_two = t22 / dist_two
    sin_two = h32 / dist_two
    coef_two = -cos_two * sin_one * beta / dist_two
    coef_one = (cos_one * beta - r12 * coef_two) / dist_one
    solution = (z_one * coef_one + z_two * coef_two).astype(jnp.bfloat16)
    residual_estimate = jnp.abs(sin_one * sin_two)
    return (solution[None], residual_estimate)


def solution(mesh):
    return jax.shard_map(
        per_device,
        mesh=mesh,
        in_specs=(
            P("sub", None, None),
            P("sub", None),
            P("sub", "crs", None),
            P("sub", None, None),
            P("sub"),
            P("sub", None, None),
            P("crs", None),
        ),
        out_specs=(P("sub", None, None), P()),
        check_vma=False,
    )
```

profile of v0, /device:TPU:1, one launch (start us, length us, event | category | flops | bytes accessed | tf_op | source)
XLA Modules:
  0.0 1146.3 jit_solution(10813083761868839373)
XLA Ops:
  9.6 128.0 %psum.56 = f32[512]{0:T(512)S(1)} all-reduce(f32[512]{0:T(512)S(1)} %fusion.2), channel_id=1, replica_groups=mesh['sub'=64,'crs'=4] {'sub'}, use_global_device_ids=true, to_apply=%region_1.2 | all-reduce | flops 512 | bytes 4096 | tf_op jit(solution)/shard_map/psum | solution.py:56
  145.7 72.4 %all-gather.7.cloned.1.call-done = bf16[2048,512]{1,0:T(8,128)(2,1)} async-done(((bf16[32,512]{1,0:T(8,128)(2,1)}), bf16[2048,512]{1,0:T(8,128)(2,1)}) %all-gather.7.cloned.1.call-update) | async-done | bytes 2097168 | tf_op jit(solution)/shard_map/all_gather | solution.py:97
  220.3 13.3 %psum.57 = bf16[32,512]{1,0:T(8,128)(2,1)S(1)} all-reduce(bf16[32,512]{1,0:T(8,128)(2,1)S(1)} %fusion.40), channel_id=1, replica_groups=mesh['sub'=64,'crs'=4] {'crs'}, use_global_device_ids=true, to_apply=%region_2.3 | all-reduce | flops 16384 | bytes 65536 | tf_op jit(solution)/shard_map/psum | solution.py:22
  233.6 19.9 %all-gather.5.cloned.1.call-done = bf16[2304,512]{1,0:T(8,128)(2,1)} async-done(((bf16[576,512]{1,0:T(8,128)(2,1)}), bf16[2304,512]{1,0:T(8,128)(2,1)}) %all-gather.5.cloned.1.call-update) | async-done | bytes 2359312 | tf_op jit(solution)/shard_map/all_gather | solution.py:90
  258.2 7.2 gather_fusion
  278.8 5.1 fusion.63
  287.4 11.8 %scatter_custom_fusion = f32[2304,512]{1,0:T(8,128)} fusion(f32[2304,512]{1,0:T(8,128)} %bitcast.96, s32[576]{0:T(1024)S(1)} %get-tuple-element.4, f32[1,576,512]{2,1,0:T(8,128)} %collective-permute-done, f32[]{:T(128)} %constant.66.clone.1), kind=kCustom, calls=%fused_computation.45 | custom fusion | flops 589824 | bytes 5898752 | tf_op jit(solution)/shard_map/scatter-add | solution.py:47
  299.3 11.8 %scatter_custom_fusion.1 = f32[2304,512]{1,0:T(8,128)} fusion(f32[2304,512]{1,0:T(8,128)} %scatter_custom_fusion, s32[576]{0:T(1024)S(1)} %get-tuple-element.3, f32[1,576,512]{2,1,0:T(8,128)} %collective-permute-done.1, f32[]{:T(128)} %constant.66.clone.1), kind=kCustom, calls=%fused_computation.43 | custom fusion | flops 589824 | bytes 5898752 | tf_op jit(solution)/shard_map/scatter-add | solution.py:48
  314.9 124.6 %psum.58 = f32[512]{0:T(512)S(1)} all-reduce(f32[512]{0:T(512)S(1)} %multiply_reduce_fusion.4), channel_id=1, replica_groups=mesh['sub'=64,'crs'=4] {'sub'}, use_global_device_ids=true, to_apply=%region_7.9 | all-reduce | flops 512 | bytes 4096 | tf_op jit(solution)/shard_map/psum | solution.py:52
  443.5 128.4 %psum.59 = f32[512]{0:T(512)S(1)} all-reduce(f32[512]{0:T(512)S(1)} %multiply_reduce_fusion.3), channel_id=1, replica_groups=mesh['sub'=64,'crs'=4] {'sub'}, use_global_device_ids=true, to_apply=%region_9.11 | all-reduce | flops 512 | bytes 4096 | tf_op jit(solution)/shard_map/psum | solution.py:56
  584.1 69.1 %all-gather.11.cloned.1.call-done = bf16[2048,512]{1,0:T(8,128)(2,1)} async-done(((bf16[32,512]{1,0:T(8,128)(2,1)}), bf16[2048,512]{1,0:T(8,128)(2,1)}) %all-gather.11.cloned.1.call-update) | async-done | bytes 2097168 | tf_op jit(solution)/shard_map/all_gather | solution.py:97
  655.3 13.3 %psum.60 = bf16[32,512]{1,0:T(8,128)(2,1)S(1)} all-reduce(bf16[32,512]{1,0:T(8,128)(2,1)S(1)} %fusion.41), channel_id=1, replica_groups=mesh['sub'=64,'crs'=4] {'crs'}, use_global_device_ids=true, to_apply=%region_10.12 | all-reduce | flops 16384 | bytes 65536 | tf_op jit(solution)/shard_map/psum | solution.py:22
  668.6 19.8 %all-gather.9.cloned.1.call-done = bf16[2304,512]{1,0:T(8,128)(2,1)} async-done(((bf16[576,512]{1,0:T(8,128)(2,1)}), bf16[2304,512]{1,0:T(8,128)(2,1)}) %all-gather.9.cloned.1.call-update) | async-done | bytes 2359312 | tf_op jit(solution)/shard_map/all_gather | solution.py:90
  688.4 4.8 convolution_add_fusion
  693.1 6.6 gather_fusion.1
  710.6 5.1 fusion.62
  718.9 12.0 %scatter_custom_fusion.2 = f32[2304,512]{1,0:T(8,128)} fusion(f32[2304,512]{1,0:T(8,128)} %bitcast.95, s32[576]{0:T(1024)S(1)} %get-tuple-element.4, f32[1,576,512]{2,1,0:T(8,128)} %collective-permute-done.2, f32[]{:T(128)} %constant.66.clone.1), kind=kCustom, calls=%fused_computation.41 | custom fusion | flops 589824 | bytes 5898752 | tf_op jit(solution)/shard_map/scatter-add | solution.py:47
  730.9 11.8 %scatter_custom_fusion.3 = f32[2304,512]{1,0:T(8,128)} fusion(f32[2304,512]{1,0:T(8,128)} %scatter_custom_fusion.2, s32[576]{0:T(1024)S(1)} %get-tuple-element.3, f32[1,576,512]{2,1,0:T(8,128)} %collective-permute-done.3, f32[]{:T(128)} %constant.66.clone.1), kind=kCustom, calls=%fused_computation.39 | custom fusion | flops 589824 | bytes 5898752 | tf_op jit(solution)/shard_map/scatter-add | solution.py:48
  745.7 125.1 %psum.61 = f32[512]{0:T(512)S(1)} all-reduce(f32[512]{0:T(512)S(1)} %multiply_reduce_fusion.2), channel_id=1, replica_groups=mesh['sub'=64,'crs'=4] {'sub'}, use_global_device_ids=true, to_apply=%region_15.17 | all-reduce | flops 512 | bytes 4096 | tf_op jit(solution)/shard_map/psum | solution.py:52
  870.8 4.9 multiply_reduce_fusion.1
  875.7 127.6 %psum.62 = f32[512]{0:T(512)S(1)} all-reduce(f32[512]{0:T(512)S(1)} %multiply_reduce_fusion.1), channel_id=1, replica_groups=mesh['sub'=64,'crs'=4] {'sub'}, use_global_device_ids=true, to_apply=%region_17.19 | all-reduce | flops 512 | bytes 4096 | tf_op jit(solution)/shard_map/psum | solution.py:52
  1003.3 5.2 multiply_reduce_fusion
  1008.5 124.0 %psum.63 = f32[512]{0:T(512)S(1)} all-reduce(f32[512]{0:T(512)S(1)} %multiply_reduce_fusion), channel_id=1, replica_groups=mesh['sub'=64,'crs'=4] {'sub'}, use_global_device_ids=true, to_apply=%region_19.21 | all-reduce | flops 512 | bytes 4096 | tf_op jit(solution)/shard_map/psum | solution.py:56
  1133.1 6.6 fusion.8
  (73 shorter events, 73.0 us)
Async XLA Ops:
  7.2 134.2 %copy-start = (bf16[1,576,2304]{2,1,0:T(8,128)(2,1)S(1)}, bf16[1,576,2304]{2,1,0:T(8,128)(2,1)}, u32[]{:S(2)}) copy-start(bf16[1,576,2304]{2,1,0:T(8,128)(2,1)} %param.11) | copy-start | bytes 7962628
  7.2 211.0 %all-gather.7.cloned.1.call-start = ((), (), s32[]{:S(2)}) async-start(), calls=%async_computation.1 | async-start | bytes 2129920 | tf_op jit(solution)/shard_map/all_gather | solution.py:97
  141.3 4.3 copy-start.7
  141.3 4.3 copy-start.6
  141.3 112.2 %copy-start.5 = (bf16[1,32,2304]{2,1,0:T(8,128)(2,1)S(1)}, bf16[1,32,2304]{2,1,0:T(8,128)(2,1)}, u32[]{:S(2)}) copy-start(bf16[1,32,2304]{2,1,0:T(8,128)(2,1)} %param.12) | copy-start | bytes 442372
  141.3 112.2 %all-gather.5.cloned.1.call-start = ((), (), s32[]{:S(2)}) async-start(), calls=%async_computation | async-start | bytes 2949120 | tf_op jit(solution)/shard_map/all_gather | solution.py:90
  145.5 507.7 %all-gather.11.cloned.1.call-start = ((), (), s32[]{:S(2)}) async-start(), calls=%async_computation.3 | async-start | bytes 2129920 | tf_op jit(solution)/shard_map/all_gather | solution.py:97
  269.0 18.5 %collective-permute-start = (f32[1,576,512]{2,1,0:T(8,128)}, f32[1,576,512]{2,1,0:T(8,128)}, u32[]{:S(2)}, u32[]{:S(2)}) collective-permute-start(f32[1,576,512]{2,1,0:T(8,128)} %get-tuple-element.14), channel_id=1, source_target_pairs={{0,4},{4,8},{8,12},{12,16},{16,20},{20,24},{24,28},{28,32},{32,36}... | collective-permute-start | bytes 3538952 | tf_op jit(solution)/shard_map/ppermute | solution.py:12
  272.6 26.6 %collective-permute-start.1 = (f32[1,576,512]{2,1,0:T(8,128)}, f32[1,576,512]{2,1,0:T(8,128)}, u32[]{:S(2)}, u32[]{:S(2)}) collective-permute-start(f32[1,576,512]{2,1,0:T(8,128)} %get-tuple-element.13), channel_id=1, source_target_pairs={{4,0},{8,4},{12,8},{16,12},{20,16},{24,20},{28,24},{32,28},{36,32}... | collective-permute-start | bytes 3538952 | tf_op jit(solution)/shard_map/ppermute | solution.py:15
  274.6 9.4 slice-start
  278.8 5.2 slice-start.1
  278.8 5.4 copy-start.4
  575.9 2.2 copy-start.3
  579.3 109.1 %all-gather.9.cloned.1.call-start = ((), (), s32[]{:S(2)}) async-start(), calls=%async_computation.2 | async-start | bytes 2949120 | tf_op jit(solution)/shard_map/all_gather | solution.py:90
  701.6 17.3 %collective-permute-start.2 = (f32[1,576,512]{2,1,0:T(8,128)}, f32[1,576,512]{2,1,0:T(8,128)}, u32[]{:S(2)}, u32[]{:S(2)}) collective-permute-start(f32[1,576,512]{2,1,0:T(8,128)} %get-tuple-element.12), channel_id=1, source_target_pairs={{0,4},{4,8},{8,12},{12,16},{16,20},{20,24},{24,28},{28,32},{32,36}... | collective-permute-start | bytes 3538952 | tf_op jit(solution)/shard_map/ppermute | solution.py:12
  705.3 25.6 %collective-permute-start.3 = (f32[1,576,512]{2,1,0:T(8,128)}, f32[1,576,512]{2,1,0:T(8,128)}, u32[]{:S(2)}, u32[]{:S(2)}) collective-permute-start(f32[1,576,512]{2,1,0:T(8,128)} %get-tuple-element.11), channel_id=1, source_target_pairs={{4,0},{8,4},{12,8},{16,12},{20,16},{24,20},{28,24},{32,28},{36,32}... | collective-permute-start | bytes 3538952 | tf_op jit(solution)/shard_map/ppermute | solution.py:15
  707.4 8.3 slice-start.2
  710.6 5.1 slice-start.3
  718.9 23.8 %copy-start.2 = (bf16[1,2304,512]{2,1,0:T(8,128)(2,1)S(1)}, bf16[1,2304,512]{2,1,0:T(8,128)(2,1)}, u32[]{:S(2)}) copy-start(bf16[1,2304,512]{2,1,0:T(8,128)(2,1)} %param.9) | copy-start | bytes 7077892
  1133.1 6.6 copy-start.1
Sparse Core Ops, SparseCore 0:
  141.4 76.6 all-gather.6
  220.5 32.9 all-gather.4
  579.4 73.6 all-gather.10
  655.4 32.9 all-gather.8
where the time goes:
time: 1150 us
  blocking collectives  784 us (68%)
  waiting for transfers between devices  181 us (16%)
  other arithmetic  97.9 us (9%)
  local copies, waits for them, and re-layouts  29.9 us (3%)
  matrix products  26.6 us (2%)
  between operations  14.7 us (1%)
  starting transfers between devices  11.5 us (1%)
    psum x3, blocking collectives, norm_of(): lax.psum(jnp.sum(vector_in * vector_in, axis=0), 'sub') + 1e-12  380 us
    psum x3, blocking collectives, inner_sum(): return lax.psum(jnp.sum(first_vec * second_vec, axis=0), 'sub')  377 us
    all_gather x2, waiting for transfers between devices, precondition(): lax.all_gather(coefficients, 'sub', axis=0, tiled=True)  142 us
    all_gather x2, waiting for transfers between devices, precondition(): local_whole = lax.all_gather(local_part, 'crs', axis=0, tiled=True)  39.7 us
    psum x2, blocking collectives, broadcast(): return lax.psum(block, axis)  26.6 us
    scatter-add x2, other arithmetic, apply_operator(): applied = applied.at[face_rows[0]].add(-4.0 * from_below)  23.8 us
    scatter-add x2, other arithmetic, apply_operator(): return applied.at[face_rows[1]].add(-4.0 * from_above)  23.6 us
  transfers between devices with their start and end apart: 8, of which 4 were waited for; matrix products, arithmetic and copies ran while one was open for 5% of the time, Pallas kernels for 0%

commit v1 on v0

v1 whole, which is shorter than its diff:
```python
import functools

import jax
import jax.numpy as jnp
from jax import lax
from jax.experimental import pallas as pl
from jax.experimental.pallas import tpu as pltpu
from jax.sharding import PartitionSpec as P

MESH = pl.DeviceIdType.MESH
F32 = jnp.float32
BF16 = jnp.bfloat16
LANES = 128
HALF = 256
PAD = 8


def dot(a, b):
    return jnp.dot(a, b, preferred_element_type=F32)


def twice(row_block):
    return jnp.concatenate([row_block, row_block], axis=1)


def tile_of(rows, most, unit):
    tile = unit
    for size in range(unit, most + 1, unit):
        if rows % size == 0:
            tile = size
    return tile


def kernel(
    plan,
    b_hbm,
    inv_hbm,
    cinv_hbm,
    shift_ref,
    basis_ref,
    count_ref,
    face_ref,
    sol_hbm,
    res_ref,
    bv,
    inv,
    crow,
    mbasis,
    mbasis_t,
    wide,
    shift_col,
    pick,
    place,
    local,
    zpad,
    zb,
    ubuf,
    ub16,
    pbuf,
    fsend,
    frecv,
    cg,
    co,
    rb1,
    rb2,
    ssem,
    rsem,
    lsem,
):
    nz, nx, ny = plan
    nj = 2 * nx
    subs = nz * nj
    kmax, n = basis_ref.shape
    cells = n // 3
    nq = n // ny
    hq = nq // 2
    faces = face_ref.shape[1]
    face = faces // 2

    me_s = lax.axis_index("sub")
    me_y = lax.axis_index("crs")
    core = lax.rem(me_s, 2)
    j = lax.rem(me_s, nj)
    x = j // 2
    z = me_s // nj

    def at_y(k):
        return (me_s, lax.rem(me_y + k, ny))

    def at_z(k):
        return (lax.rem(z + k, nz) * nj + j, me_y)

    def at_j(k):
        return (z * nj + lax.rem(j + k, nj), me_y)

    def at_x(k):
        return (z * nj + lax.rem(x + k, nx) * 2 + core, me_y)

    other_core = (me_s + 1 - 2 * core, me_y)
    above = (lax.rem(me_s + 1, subs), me_y)
    below = (lax.rem(me_s + subs - 1, subs), me_y)

    used = [0]
    sent = []

    def remote(src, dst, device, slot=None):
        i = used[0]
        used[0] += 1
        cp = pltpu.make_async_remote_copy(
            src_ref=src,
            dst_ref=dst,
            send_sem=ssem.at[i],
            recv_sem=rsem.at[i],
            device_id=device,
            device_id_type=MESH,
        )
        cp.start()
        sent.append(cp)
        arrived = pltpu.make_async_remote_copy(
            src_ref=src if slot is None else slot,
            dst_ref=dst if slot is None else slot,
            send_sem=ssem.at[i],
            recv_sem=rsem.at[i],
            device_id=device,
            device_id_type=MESH,
        )
        return arrived

    loads = []
    for h in range(2):
        cp = pltpu.make_async_copy(b_hbm.at[:, pl.ds(h * HALF, HALF)], bv.at[h], lsem.at[h])
        cp.start()
        loads.append(cp)
    load_inv = pltpu.make_async_copy(inv_hbm, inv, lsem.at[2])
    load_inv.start()

    barrier = pltpu.get_barrier_semaphore()
    partners = [at_y(k) for k in range(1, ny)] + [at_z(k) for k in range(1, nz)]
    partners += [at_j(k) for k in range(1, nj)] + [above, below]
    for device in partners:
        pl.semaphore_signal(barrier, inc=1, device_id=device, device_id_type=MESH)

    keep = lax.broadcasted_iota(jnp.int32, (kmax, n), 0) < count_ref[0]
    masked = jnp.where(keep, basis_ref[...].astype(F32), 0.0)
    mbasis[...] = masked.astype(BF16)
    wide[...] = jnp.zeros_like(wide)
    wide[pl.ds(0, kmax), :] = masked
    for i in range(n // LANES):
        block = wide[:, i * LANES : (i + 1) * LANES]
        mbasis_t[pl.ds(i * LANES, LANES), :] = block.T.astype(BF16)

    pl.semaphore_wait(barrier, len(partners))

    panel = cinv_hbm.shape[0]
    owner = me_s * kmax // panel
    offset = pl.multiple_of(lax.rem(me_s * kmax, panel), kmax)
    row_sem = used[0]
    used[0] += ny - 1

    def row_copy(k):
        return pltpu.make_async_remote_copy(
            src_ref=cinv_hbm.at[pl.ds(offset, kmax), :],
            dst_ref=crow,
            send_sem=ssem.at[row_sem + k - 1],
            recv_sem=rsem.at[row_sem],
            device_id=at_y(k),
            device_id_type=MESH,
        )

    own_rows = pltpu.make_async_copy(cinv_hbm.at[pl.ds(offset, kmax), :], crow, lsem.at[3])

    @pl.when(me_y == owner)
    def _():
        for k in range(1, ny):
            row_copy(k).start()
        own_rows.start()

    my_half = me_y // 2
    my_side = lax.rem(me_y, 2)

    def coarse_begin(it, field):
        part = dot(mbasis[...], field[my_half])
        own = jnp.where(my_side == 0, part[:, :LANES], part[:, LANES:])
        cg[it, z, x, core] = own.astype(BF16)
        waits = []
        for k in range(1, nz):
            mine = cg.at[it, z, x, core]
            waits.append(remote(mine, mine, at_z(k), cg.at[it, lax.rem(z + nz - k, nz), x, core]))
        return waits

    def coarse_x(it, waits):
        for w in waits:
            w.wait_recv()
        out = []
        for k in range(1, nx):
            mine = cg.at[it, :, x, core]
            out.append(remote(mine, mine, at_x(k), cg.at[it, :, lax.rem(x + nx - k, nx), core]))
        return out

    def coarse_core(it, waits):
        for w in waits:
            w.wait_recv()
        mine = cg.at[it, :, :, core]
        return remote(mine, mine, other_core, cg.at[it, :, :, 1 - core])

    def coarse_end(it, wait):
        wait.wait_recv()
        stacked = cg[it].reshape(subs * kmax, LANES)
        co[it, me_y] = dot(crow[...], stacked).astype(BF16)
        waits = []
        for k in range(1, ny):
            mine = co.at[it, me_y]
            waits.append(remote(mine, mine, at_y(k), co.at[it, lax.rem(me_y + ny - k, ny)]))
        return waits

    base = pl.multiple_of(me_y * nq, nq)
    right, left = at_y(1), at_y(ny - 1)

    def part_rows(k, low):
        owner_y = lax.rem(me_y + k, ny)
        return pl.ds(pl.multiple_of(owner_y * nq + (0 if low else hq), hq), hq)

    def local_product(it, h, field):
        tile = tile_of(nq, 288, 16)

        @pl.loop(0, nq // tile)
        def _(i):
            rows = pl.ds(pl.multiple_of(i * tile, tile), tile)
            out = dot(inv[rows, :], field[h])
            local[it, h, pl.ds(pl.multiple_of(base + i * tile, 16), tile), :] = out.astype(BF16)

    def gather_begin(it, h):
        buf = local.at[it, h]

        def send(k, low, device):
            mine = buf.at[part_rows(0, low), :]
            return remote(mine, mine, device, buf.at[part_rows(k, low), :])

        from_left_low = send(ny - 1, True, right)
        from_right_high = send(1, False, left)
        from_left_high = send(ny - 1, False, right)
        from_right_low = send(1, True, left)
        return from_left_low, from_right_high, from_left_high, from_right_low

    def gather_forward(it, h, waits):
        buf = local.at[it, h]
        waits[0].wait_recv()
        low = buf.at[part_rows(ny - 1, True), :]
        far_low = remote(low, low, right, buf.at[part_rows(2, True), :])
        waits[1].wait_recv()
        high = buf.at[part_rows(1, False), :]
        far_high = remote(high, high, left, buf.at[part_rows(2, False), :])
        return waits[2], waits[3], far_low, far_high

    def assemble(it, h):
        top = jnp.concatenate([co[it, 2 * h], co[it, 2 * h + 1]], axis=1)
        coarse = jnp.concatenate([top, jnp.zeros((LANES - kmax, HALF), BF16)], axis=0)
        tile = tile_of(cells, 256, 16)
        per = cells // tile

        @pl.loop(0, 3 * per)
        def _(i):
            comp = i // per
            rows = pl.ds(pl.multiple_of(i * tile, tile), tile)
            value = local[it, h, rows, :].astype(F32) + dot(mbasis_t[rows, :], coarse)
            start = pl.multiple_of(lax.rem(i, per) * tile + PAD, PAD)
            zpad[it, h, comp, pl.ds(start, tile), :] = value
            zb[rows, :] = value.astype(BF16)

    def faces_begin(it, h):
        tile = tile_of(faces, 288, 16)

        @pl.loop(0, faces // tile)
        def _(i):
            rows = pl.ds(pl.multiple_of(i * tile, tile), tile)
            fsend[it, h, rows, :] = dot(pick[rows, :], zb[...]).astype(BF16)

        lower, upper = pl.ds(0, face), pl.ds(face, face)
        from_below = remote(
            fsend.at[it, h, upper, :], frecv.at[it, h, lower, :], above, frecv.at[it, h, lower, :]
        )
        from_above = remote(
            fsend.at[it, h, lower, :], frecv.at[it, h, upper, :], below, frecv.at[it, h, upper, :]
        )
        return from_below, from_above

    def stencil(it, h, waits, h11):
        for w in waits:
            w.wait_recv()
        tile = tile_of(n, 256, 16)

        @pl.loop(0, n // tile)
        def _(i):
            rows = pl.ds(pl.multiple_of(i * tile, tile), tile)
            pbuf[rows, :] = dot(place[rows, :], frecv[it, h])

        size = tile_of(cells, 32, 16)

        def fold(value):
            return jnp.sum(value.reshape(size // 8, 8, HALF), axis=0)

        def step(i, sums):
            m0 = pl.multiple_of(i * size, size)
            blocks = [
                zpad[it, h, comp, pl.ds(m0, size + 2 * PAD), :] for comp in range(3)
            ]
            mid = [block[PAD : PAD + size] for block in blocks]
            total = mid[0] + mid[1] + mid[2]
            s0, s1, s2 = sums
            for comp in range(3):
                rows = pl.ds(pl.multiple_of(comp * cells + m0, size), size)
                value = (6.5 + twice(shift_col[rows, :])) * mid[comp] - 0.5 * total
                value -= blocks[comp][PAD - 1 : PAD - 1 + size]
                value -= blocks[comp][PAD + 1 : PAD + 1 + size]
                value -= 4.0 * pbuf[rows, :]
                b = bv[h, rows, :].astype(F32)
                if it == 0:
                    ubuf[h, rows, :] = value
                    ub16[h, rows, :] = value.astype(BF16)
                    s0, s1, s2 = s0 + fold(b * b), s1 + fold(value * b), s2 + fold(value * value)
                else:
                    u = ubuf[h, rows, :]
                    g = value - h11 * u
                    t = u - h11 * b
                    s0, s1, s2 = s0 + fold(g * b), s1 + fold(g * t), s2 + fold(g * g)
            return s0, s1, s2

        zero = jnp.zeros((8, HALF), F32)
        sums = lax.fori_loop(0, cells // size, step, (zero, zero, zero))
        rows = []
        for value in sums:
            row = jnp.sum(value, axis=0, keepdims=True)
            rows += [row[:, :LANES], row[:, LANES:]]
        return jnp.concatenate(rows + [jnp.zeros((2, LANES), F32)], axis=0)

    def reduce_begin(it, h, partial):
        rb1[it, h, j] = partial
        mine = rb1.at[it, h, j]
        return [
            remote(mine, mine, at_j(k), rb1.at[it, h, lax.rem(j + nj - k, nj)]) for k in range(1, nj)
        ]

    def reduce_z(it, h, waits):
        for w in waits:
            w.wait_recv()
        rb2[it, h, z] = jnp.sum(rb1[it, h], axis=0)
        mine = rb2.at[it, h, z]
        return [
            remote(mine, mine, at_z(k), rb2.at[it, h, lax.rem(z + nz - k, nz)]) for k in range(1, nz)
        ]

    def reduce_end(it, h, waits):
        for w in waits:
            w.wait_recv()
        total = jnp.sum(rb2[it, h], axis=0)
        return [
            jnp.concatenate([total[2 * i : 2 * i + 1], total[2 * i + 1 : 2 * i + 2]], axis=1)
            for i in range(3)
        ]

    for cp in loads:
        cp.wait()
    coarse_wait = coarse_begin(0, bv)
    load_inv.wait()
    local_product(0, 0, bv)
    g00 = gather_begin(0, 0)
    local_product(0, 1, bv)

    zero_rows = jnp.zeros((PAD, HALF), F32)
    for it in range(2):
        for h in range(2):
            for comp in range(3):
                zpad[it, h, comp, pl.ds(0, PAD), :] = zero_rows
                zpad[it, h, comp, pl.ds(cells + PAD, PAD), :] = zero_rows

    for i in range(n // LANES):
        row = jnp.broadcast_to(shift_ref[:, i * LANES : (i + 1) * LANES], (LANES, LANES))
        shift_col[pl.ds(i * LANES, LANES), :] = row.T

    coarse_wait = coarse_x(0, coarse_wait)

    lane = lax.broadcasted_iota(jnp.int32, (LANES, LANES), 1)
    line = lax.broadcasted_iota(jnp.int32, (LANES, LANES), 0)
    for i in range(faces // LANES):
        row = jnp.broadcast_to(face_ref[:, i * LANES : (i + 1) * LANES], (LANES, LANES))
        column = row.astype(F32).T.astype(jnp.int32)
        for k in range(n // LANES):
            hit = jnp.where(column == lane + k * LANES, 1.0, 0.0)
            pick[pl.ds(i * LANES, LANES), k * LANES : (k + 1) * LANES] = hit.astype(BF16)

    g00 = gather_forward(0, 0, g00)
    g01 = gather_begin(0, 1)
    coarse_wait = coarse_core(0, coarse_wait)

    for i in range(faces // LANES):
        row = jnp.broadcast_to(face_ref[:, i * LANES : (i + 1) * LANES], (LANES, LANES))
        slot = lane + i * LANES
        missing = ((slot < face) & (me_s == 0)) | ((slot >= face) & (me_s == subs - 1))
        row = jnp.where(missing, -1, row)
        for k in range(n // LANES):
            hit = jnp.where(row == line + k * LANES, 1.0, 0.0)
            place[pl.ds(k * LANES, LANES), i * LANES : (i + 1) * LANES] = hit.astype(BF16)

    @pl.when(me_y == owner)
    def _():
        own_rows.wait()
        for k in range(1, ny):
            row_copy(k).wait_send()

    @pl.when(me_y != owner)
    def _():
        row_copy(1).wait_recv()

    coarse_wait = coarse_end(0, coarse_wait)
    for w in coarse_wait:
        w.wait_recv()
    for w in g00:
        w.wait_recv()
    assemble(0, 0)
    f00 = faces_begin(0, 0)
    g01 = gather_forward(0, 1, g01)
    p00 = stencil(0, 0, f00, None)
    r00 = reduce_begin(0, 0, p00)
    local_product(1, 0, ub16)
    g10 = gather_begin(1, 0)
    for w in g01:
        w.wait_recv()
    assemble(0, 1)
    f01 = faces_begin(0, 1)
    g10 = gather_forward(1, 0, g10)
    r00 = reduce_z(0, 0, r00)
    p01 = stencil(0, 1, f01, None)
    r01 = reduce_begin(0, 1, p01)
    coarse_wait = coarse_begin(1, ub16)
    local_product(1, 1, ub16)
    g11 = gather_begin(1, 1)
    r01 = reduce_z(0, 1, r01)
    coarse_wait = coarse_x(1, coarse_wait)
    sums1 = [reduce_end(0, 0, r00), None]
    coarse_wait = coarse_core(1, coarse_wait)
    sums1[1] = reduce_end(0, 1, r01)
    coarse_wait = coarse_end(1, coarse_wait)
    g11 = gather_forward(1, 1, g11)

    scalars = []
    for bb, ub, uu in sums1:
        beta2 = bb + 1e-12
        beta = jnp.sqrt(beta2)
        h11 = ub / beta2
        h21s = jnp.maximum((uu - h11 * (2.0 * ub - h11 * bb)) / beta2, 0.0) + 1e-12
        scalars.append((bb, beta2, beta, h11, h21s, jnp.sqrt(h21s)))

    for w in coarse_wait:
        w.wait_recv()
    for w in g10:
        w.wait_recv()
    assemble(1, 0)
    f10 = faces_begin(1, 0)
    p10 = stencil(1, 0, f10, scalars[0][3])
    r10 = reduce_begin(1, 0, p10)
    for w in g11:
        w.wait_recv()
    assemble(1, 1)
    f11 = faces_begin(1, 1)
    r10 = reduce_z(1, 0, r10)
    p11 = stencil(1, 1, f11, scalars[1][3])
    r11 = reduce_begin(1, 1, p11)

    def finish(h, sums):
        bb, beta2, beta, h11, h21s, h21 = scalars[h]
        gb, gt, gg = sums
        scale = 1.0 / (beta * h21)
        h12 = gb * scale / beta
        h22 = gt * scale * scale
        ww = gg * scale * scale
        ff_gap = 1e-12 / beta2
        ss_gap = 1e-12 / h21s
        fs = h11 * ff_gap / h21
        h32s = ww - h12 * h12 * (1.0 + ff_gap) - h22 * h22 * (1.0 + ss_gap) + 2.0 * h12 * h22 * fs
        h32 = jnp.sqrt(jnp.maximum(h32s, 0.0) + 1e-12)
        dist_one = jnp.sqrt(h11 * h11 + h21 * h21)
        cos_one = h11 / dist_one
        sin_one = h21 / dist_one
        r12 = cos_one * h12 + sin_one * h22
        t22 = cos_one * h22 - sin_one * h12
        dist_two = jnp.sqrt(t22 * t22 + h32 * h32)
        cos_two = t22 / dist_two
        sin_two = h32 / dist_two
        y2 = -cos_two * sin_one * beta / dist_two
        y1 = (cos_one * beta - r12 * y2) / dist_one
        weight_two = y2 * scale
        weight_one = y1 / beta - h11 * weight_two
        res_ref[:, h * HALF : (h + 1) * HALF] = jnp.abs(sin_one * sin_two)
        size = tile_of(cells, 64, 16)
        per = cells // size

        @pl.loop(0, 3 * per)
        def _(i):
            comp = i // per
            start = pl.multiple_of(lax.rem(i, per) * size + PAD, PAD)
            one = zpad[0, h, comp, pl.ds(start, size), :]
            two = zpad[1, h, comp, pl.ds(start, size), :]
            rows = pl.ds(pl.multiple_of(i * size, size), size)
            bv[h, rows, :] = (one * weight_one + two * weight_two).astype(BF16)

        out = pltpu.make_async_copy(bv.at[h], sol_hbm.at[:, pl.ds(h * HALF, HALF)], lsem.at[4 + h])
        out.start()
        return out

    r10 = reduce_end(1, 0, r10)
    out0 = finish(0, r10)
    r11 = reduce_z(1, 1, r11)
    r11 = reduce_end(1, 1, r11)
    out1 = finish(1, r11)
    for cp in sent:
        cp.wait_send()
    out0.wait()
    out1.wait()


def count_copies(nz, nx, ny):
    nj = 2 * nx
    coarse = 2 * ((nz - 1) + (nx - 1) + 1 + (ny - 1))
    return (ny - 1) + coarse + 4 * 6 + 4 * 2 + 4 * ((nj - 1) + (nz - 1))


def per_device(nz, nx, right_sides, shift, inverses, basis, counts, face_rows, coarse_inverse):
    ny = lax.axis_size("crs")
    n, width = right_sides.shape[1:]
    nq = n // ny
    kmax = basis.shape[1]
    faces = 2 * face_rows.shape[2]
    cells = n // 3
    nj = 2 * nx
    subs = nz * nj
    copies = count_copies(nz, nx, ny)
    any_spec = pl.BlockSpec(memory_space=pl.ANY)
    vmem = pl.BlockSpec(memory_space=pltpu.VMEM)
    out, residual = pl.pallas_call(
        functools.partial(kernel, (nz, nx, ny)),
        out_shape=(
            jax.ShapeDtypeStruct((n, width), BF16),
            jax.ShapeDtypeStruct((1, width), F32),
        ),
        in_specs=[
            any_spec,
            any_spec,
            any_spec,
            vmem,
            vmem,
            pl.BlockSpec(memory_space=pltpu.SMEM),
            vmem,
        ],
        out_specs=(any_spec, vmem),
        scratch_shapes=[
            pltpu.VMEM((2, n, HALF), BF16),
            pltpu.VMEM((nq, n), BF16),
            pltpu.VMEM((kmax, subs * kmax), BF16),
            pltpu.VMEM((kmax, n), BF16),
            pltpu.VMEM((n, LANES), BF16),
            pltpu.VMEM((LANES, n), F32),
            pltpu.VMEM((n, LANES), F32),
            pltpu.VMEM((faces, n), BF16),
            pltpu.VMEM((n, faces), BF16),
            pltpu.VMEM((2, 2, n, HALF), BF16),
            pltpu.VMEM((2, 2, 3, cells + 2 * PAD, HALF), F32),
            pltpu.VMEM((n, HALF), BF16),
            pltpu.VMEM((2, n, HALF), F32),
            pltpu.VMEM((2, n, HALF), BF16),
            pltpu.VMEM((n, HALF), F32),
            pltpu.VMEM((2, 2, faces, HALF), BF16),
            pltpu.VMEM((2, 2, faces, HALF), BF16),
            pltpu.VMEM((2, nz, nx, 2, kmax, LANES), BF16),
            pltpu.VMEM((2, ny, kmax, LANES), BF16),
            pltpu.VMEM((2, 2, nj, 8, LANES), F32),
            pltpu.VMEM((2, 2, nz, 8, LANES), F32),
            pltpu.SemaphoreType.DMA((copies,)),
            pltpu.SemaphoreType.DMA((copies,)),
            pltpu.SemaphoreType.DMA((6,)),
        ],
        compiler_params=pltpu.CompilerParams(
            collective_id=0, has_side_effects=True, vmem_limit_bytes=60 * 1024 * 1024
        ),
    )(
        right_sides[0],
        inverses[0],
        coarse_inverse,
        shift,
        basis[0],
        counts,
        face_rows.reshape(1, faces),
    )
    return out[None], residual.reshape(width)


def solution(mesh):
    subs = mesh.shape["sub"]
    nz = 8 if subs == 64 else 2
    nx = subs // (2 * nz)
    return jax.shard_map(
        functools.partial(per_device, nz, nx),
        mesh=mesh,
        in_specs=(
            P("sub", None, None),
            P("sub", None),
            P("sub", "crs", None),
            P("sub", None, None),
            P("sub"),
            P("sub", None, None),
            P("crs", None),
        ),
        out_specs=(P("sub", None, None), P()),
        check_vma=False,
    )
```

time: 1150 us -> 127 us (0.11)
  blocking collectives: 784 us -> 0 us
  waiting for transfers between devices: 181 us -> 0 us
  Pallas kernels: 0 us -> 120 us
  other arithmetic: 97.9 us -> 0 us
  matrix products: 26.6 us -> 0 us
  local copies, waits for them, and re-layouts: 29.9 us -> 5.17 us
  between operations: 14.7 us -> 1.29 us
  starting transfers between devices: 11.5 us -> 0 us
    psum x8 -> x0, blocking collectives: 784 us -> none  [the longest x3 380 us: norm_of(): lax.psum(jnp.sum(vector_in * vector_in, axis=0), 'sub') + 1e-12]
    all_gather x4 -> x0, waiting for transfers between devices: 181 us -> none  [the longest x2 142 us: precondition(): lax.all_gather(coefficients, 'sub', axis=0, tiled=True)]
    pallas_call x0 -> x1, Pallas kernels: none -> 120 us  [per_device(): pl.pallas_call(functools.partial(kernel, (nz, nx, ny)), out_shape=(jax.Sh...]
    scatter-add x4 -> x0, other arithmetic: 47.4 us -> none  [the longest x2 23.8 us: apply_operator(): applied = applied.at[face_rows[0]].add(-4.0 * from_below)]
    reduce_sum x8 -> x0, other arithmetic: 30.7 us -> none  [the longest x3 11.7 us: inner_sum(): return lax.psum(jnp.sum(first_vec * second_vec, axis=0), 'sub')]
    dot_general x8 -> x0, matrix products: 26.6 us -> none  [the longest x2 9.47 us: precondition(): lax.dot_general(masked_basis, coarse_values, (((0,), (0,)), ((), ())), pr...]
    gather x2 -> x0, local copies, waits for them, and re-layouts: 13.8 us -> none  [neighbour_rims(): jnp.take(vector_in, face_rows.reshape(-1), axis=0)]
    slice x4 -> x0, local copies, waits for them, and re-layouts: 13.5 us -> none  [the longest x2 10.2 us: apply_operator(): below_cells = jnp.concatenate([zero_column, component_grid[:, :-1]], axis=1)]
  transfers between devices with their start and end apart: 8 -> 0, of which waited for: 4 -> 0; matrix products, arithmetic and copies ran while one was open for 5% -> 0% of each run, Pallas kernels for 0% -> 0%
where the time goes in v1:
time: 127 us; the launch traced here: 126 us
  Pallas kernels  120 us (94%)
  local copies, waits for them, and re-layouts  5.17 us (4%)
  between operations  1.29 us (1%)
    pallas_call x1, Pallas kernels, per_device(): pl.pallas_call(functools.partial(kernel, (nz, nx, ny)), out_shape=(jax.Sh...  120 us
    unnamed x4, local copies, waits for them, and re-layouts  3.81 us

profile of v1, /device:TPU:1, one launch (start us, length us, event | category | flops | bytes accessed | tf_op | source)
XLA Modules:
  0.0 126.5 jit_solution(6803659043033744592)
XLA Ops:
  1.3 1.4 %reshape.10.face_ref = s32[1,1152]{1,0:T(1,128)} reshape(s32[1,2,576]{2,1,0:T(2,128)} %param.12) | data formatting | bytes 9216 | tf_op jit(solution)/shard_map/reshape | solution.py:591
  2.6 120.0 %shard_map.86 = (bf16[2304,512]{1,0:T(8,128)(2,1)}, f32[1,512]{1,0:T(1,128)}) custom-call(bf16[2304,512]{1,0:T(8,128)(2,1)} %bitcast.7, bf16[576,2304]{1,0:T(8,128)(2,1)} %bitcast.5, bf16[512,2048]{1,0:T(8,128)(2,1)} %cinv_hbm.1, f32[1,2304]{1,0:T(1,128)} %shift_ref.1, bf16[32,2304]{1,0:T(8,128)(2,1)} %bitcast.8, s32[1]{0:T(128)S(6)} %copy.11.count_ref, ...), custom_call_target="tpu_custom_call" | custom-call | tf_op jit(solution)/shard_map/pallas_call | solution.py:539
  122.7 0.0 copy-start
  122.7 3.2 %copy.12 = bf16[1,2304,512]{2,1,0:T(8,128)(2,1)} copy(bf16[1,2304,512]{2,1,0:T(8,128)(2,1)} %bitcast.6) | data formatting | bytes 4718592
  125.9 0.0 copy-done
  125.9 0.6 copy.13
Async XLA Ops:
  122.7 3.2 %copy-start = (f32[1,512]{1,0:T(1,128)S(1)}, f32[1,512]{1,0:T(1,128)}, u32[]{:S(2)}) copy-start(f32[1,512]{1,0:T(1,128)} %get-tuple-element.5) | copy-start | bytes 6148

commit v2 on v0

v2 whole, which is shorter than its diff:
```python
import functools

import jax
import jax.numpy as jnp
from jax import lax
from jax.experimental import pallas as pl
from jax.experimental.pallas import tpu as pltpu
from jax.sharding import PartitionSpec as P

MESH = pl.DeviceIdType.MESH
F32 = jnp.float32
BF16 = jnp.bfloat16
LANES = 128
HALF = 256
PAD = 8


def dot(a, b):
    return jnp.dot(a, b, preferred_element_type=F32)


def twice(block):
    return jnp.concatenate([block, block], axis=1)


def tile_of(rows, most, unit):
    tile = unit
    for size in range(unit, most + 1, unit):
        if rows % size == 0:
            tile = size
    return tile


def kernel(
    plan,
    b_hbm,
    inv_hbm,
    cinv_hbm,
    shift_ref,
    basis_ref,
    count_ref,
    face_ref,
    sol_hbm,
    res_ref,
    bv,
    inv,
    basis_t,
    wide,
    shift_col,
    pick,
    place,
    inv_place,
    acc,
    local,
    prio,
    zpad,
    zb,
    ubuf,
    ub16,
    fsend,
    frecv,
    zq,
    zbq,
    yq,
    uq,
    fsend_q,
    frecv_q,
    crows,
    select,
    cpart,
    coef,
    cg,
    cpsend,
    cprecv,
    co,
    rb1,
    rb2,
    weights,
    ssem,
    rsem,
    lsem,
):
    nz, nx, ny = plan
    nj = 2 * nx
    subs = nz * nj
    kmax, n = basis_ref.shape
    cells = n // 3
    nq = n // ny
    hq = nq // 2
    face = face_ref.shape[1]
    faces = 2 * face

    me_s = lax.axis_index("sub")
    me_y = lax.axis_index("crs")
    j = lax.rem(me_s, nj)
    z = me_s // nj
    my_half = me_y // 2
    my_side = lax.rem(me_y, 2)

    def at_y(k):
        return (me_s, lax.rem(me_y + k, ny))

    def at_z(k):
        return (lax.rem(z + k, nz) * nj + j, me_y)

    def at_j(k):
        return (z * nj + lax.rem(j + k, nj), me_y)

    above = (lax.rem(me_s + 1, subs), me_y)
    below = (lax.rem(me_s + subs - 1, subs), me_y)

    def side(block):
        return jnp.where(my_side == 0, block[:, :LANES], block[:, LANES:])

    used = [0]
    sent = []

    def describe(i, src, dst, device):
        return pltpu.make_async_remote_copy(
            src_ref=src,
            dst_ref=dst,
            send_sem=ssem.at[i],
            recv_sem=rsem.at[i],
            device_id=device,
            device_id_type=MESH,
        )

    def remote(src, dst, device, slot):
        i = used[0]
        used[0] += 1
        cp = describe(i, src, dst, device)
        cp.start()
        sent.append(cp)
        arrived = describe(i, slot, slot, device)
        return arrived

    def wait_all(waits):
        for w in waits:
            w.wait_recv()

    ext = nq + kmax
    cut = ext // 2
    tiles = ((0, cut), (cut, ext - cut))

    def load_b(h):
        return pltpu.make_async_copy(b_hbm.at[:, pl.ds(h * HALF, HALF)], bv.at[h], lsem.at[h])

    def load_inv(i):
        rows = pl.ds(tiles[i][0], min(tiles[i][1], nq - tiles[i][0]))
        return pltpu.make_async_copy(inv_hbm.at[rows, :], inv.at[rows, :], lsem.at[2 + i])

    loads = [load_b(0), load_inv(0), load_inv(1), load_b(1)]
    for cp in loads:
        cp.start()

    barrier = pltpu.get_barrier_semaphore()
    partners = [at_y(k) for k in range(1, ny)] + [at_z(k) for k in range(1, nz)]
    partners += [at_j(k) for k in range(1, nj)] + [above, below]
    for device in partners:
        pl.semaphore_signal(barrier, inc=1, device_id=device, device_id_type=MESH)

    panel = cinv_hbm.shape[0]
    line_rows = nj * kmax
    owner = z * line_rows // panel
    offset = pl.multiple_of(lax.rem(z * line_rows, panel), line_rows)
    own_rows = pltpu.make_async_copy(cinv_hbm.at[pl.ds(offset, line_rows), :], crows, lsem.at[4])

    @pl.when(me_y == owner)
    def _():
        own_rows.start()

    keep = lax.broadcasted_iota(jnp.int32, (kmax, n), 0) < count_ref[0]
    masked = jnp.where(keep, basis_ref[...].astype(F32), 0.0)
    inv[pl.ds(nq, kmax), :] = masked.astype(BF16)
    wide[...] = jnp.zeros_like(wide)
    wide[pl.ds(0, kmax), :] = masked

    @pl.when(me_y == owner)
    def _():
        at = lax.broadcasted_iota(jnp.int32, select.shape, 0)
        col = lax.broadcasted_iota(jnp.int32, select.shape, 1)
        wanted = (col // kmax) * line_rows + j * kmax + lax.rem(col, kmax)
        select[...] = jnp.where(at == wanted, 1.0, 0.0).astype(BF16)
        own_rows.wait()
        cpart[...] = dot(crows[...], select[...]).astype(BF16)

    pl.semaphore_wait(barrier, len(partners))

    part_sem = used[0]
    used[0] += ny - 1

    def part_copy(k):
        return pltpu.make_async_remote_copy(
            src_ref=cpart,
            dst_ref=cpart,
            send_sem=ssem.at[part_sem + k - 1],
            recv_sem=rsem.at[part_sem],
            device_id=at_y(k),
            device_id_type=MESH,
        )

    def part_begin():
        @pl.when(me_y == owner)
        def _():
            for k in range(1, ny):
                part_copy(k).start()

    def part_end():
        @pl.when(me_y == owner)
        def _():
            for k in range(1, ny):
                part_copy(k).wait_send()

        @pl.when(me_y != owner)
        def _():
            part_copy(1).wait_recv()

    def coarse_begin(it):
        cg[it, z] = side(coef[it, my_half]).astype(BF16)
        mine = cg.at[it, z]
        return [
            remote(mine, mine, at_z(k), cg.at[it, lax.rem(z + nz - k, nz)]) for k in range(1, nz)
        ]

    def coarse_line(it, waits):
        wait_all(waits)
        partial = dot(cpart[...], cg[it].reshape(nz * kmax, LANES))
        cpsend[it] = partial.reshape(nj, kmax, LANES)
        cprecv[it, j] = cpsend[it, j]
        return [
            remote(
                cpsend.at[it, lax.rem(j + k, nj)],
                cprecv.at[it, j],
                at_j(k),
                cprecv.at[it, lax.rem(j + nj - k, nj)],
            )
            for k in range(1, nj)
        ]

    def coarse_end(it, waits):
        wait_all(waits)
        co[it, me_y] = jnp.sum(cprecv[it], axis=0).astype(BF16)
        mine = co.at[it, me_y]
        return [
            remote(mine, mine, at_y(k), co.at[it, lax.rem(me_y + ny - k, ny)])
            for k in range(1, ny)
        ]

    base = pl.multiple_of(me_y * nq, nq)
    right, left = at_y(1), at_y(ny - 1)

    def part_rows(k, low):
        owner_y = lax.rem(me_y + k, ny)
        return pl.ds(pl.multiple_of(owner_y * nq + (0 if low else hq), hq), hq)

    def keep_product(it, h, start, size, out):
        rows = min(size, nq - start)
        local[it, h, pl.ds(pl.multiple_of(base + start, 16), rows), :] = out[:rows].astype(BF16)
        if rows < size:
            coef[it, h] = out[rows:]

    def first_product(h, ready=None):
        for i, (start, size) in enumerate(tiles):
            if ready is not None:
                ready(i)
            keep_product(0, h, start, size, dot(inv[pl.ds(start, size), :], bv[h]))

    def second_product(h):
        for start, size in tiles:
            acc[pl.ds(start, size), :] = dot(inv[pl.ds(start, size), :], ub16[...])

    def second_faces(h, waits):
        wait_all(waits)
        for start, size in tiles:
            rows = pl.ds(start, size)
            out = acc[rows, :] - 4.0 * dot(inv_place[rows, :], frecv[h])
            keep_product(1, h, start, size, out)

    def gather_begin(it, h, first):
        buf = local.at[it, h]

        def send(k, low, device):
            mine = buf.at[part_rows(0, low), :]
            return remote(mine, mine, device, buf.at[part_rows(k, low), :])

        if first:
            return send(ny - 1, True, right), send(1, False, left)
        return send(ny - 1, False, right), send(1, True, left)

    def gather_forward(it, h, waits):
        buf = local.at[it, h]
        waits[0].wait_recv()
        low = buf.at[part_rows(ny - 1, True), :]
        far_low = remote(low, low, right, buf.at[part_rows(2, True), :])
        waits[1].wait_recv()
        high = buf.at[part_rows(1, False), :]
        far_high = remote(high, high, left, buf.at[part_rows(2, False), :])
        return far_low, far_high

    def padded(block):
        rest = jnp.zeros((LANES - kmax, block.shape[1]), BF16)
        return jnp.concatenate([block, rest], axis=0)

    def coarse_half(it, h):
        return padded(jnp.concatenate([co[it, 2 * h], co[it, 2 * h + 1]], axis=1))

    def assemble(h):
        coarse = coarse_half(0, h)
        tile = tile_of(cells, 768, 16)
        per = cells // tile

        @pl.loop(0, 3 * per)
        def _(i):
            comp = i // per
            rows = pl.ds(pl.multiple_of(i * tile, tile), tile)
            value = local[0, h, rows, :].astype(F32) + dot(basis_t[rows, :], coarse)
            start = pl.multiple_of(lax.rem(i, per) * tile + PAD, PAD)
            zpad[h, comp, pl.ds(start, tile), :] = value
            zb[rows, :] = value.astype(BF16)

    def assemble_quarter(field):
        coarse = padded(co[1, me_y])
        tile = tile_of(cells, 768, 16)
        per = cells // tile

        @pl.loop(0, 3 * per)
        def _(i):
            comp = i // per
            rows = pl.ds(pl.multiple_of(i * tile, tile), tile)
            value = field(rows).astype(F32) + dot(basis_t[rows, :], coarse)
            start = pl.multiple_of(lax.rem(i, per) * tile + PAD, PAD)
            zq[comp, pl.ds(start, tile), :] = value
            zbq[rows, :] = value.astype(BF16)

    lower, upper = pl.ds(0, face), pl.ds(face, face)

    def faces_begin(field, out, into):
        tile = tile_of(face, 288, 16)
        waits = []
        for start in range(0, face, tile):
            for first, other, device in ((face, 0, above), (0, face, below)):
                rows, there = pl.ds(first + start, tile), pl.ds(other + start, tile)
                out[rows, :] = dot(pick[rows, :], field[...]).astype(BF16)
                waits.append(
                    remote(out.at[rows, :], into.at[there, :], device, into.at[there, :])
                )
        return waits

    def stencil(load, shift_of, store):
        size = tile_of(cells, 32, 16)

        @pl.loop(0, cells // size)
        def _(i):
            m0 = pl.multiple_of(i * size, size)
            blocks = [load(comp, pl.ds(m0, size + 2 * PAD)) for comp in range(3)]
            mid = [block[PAD : PAD + size] for block in blocks]
            total = 0.5 * (mid[0] + mid[1] + mid[2])
            for comp in range(3):
                rows = pl.ds(pl.multiple_of(comp * cells + m0, size), size)
                value = (6.5 + shift_of(rows)) * mid[comp] - total
                value -= blocks[comp][PAD - 1 : PAD - 1 + size]
                value -= blocks[comp][PAD + 1 : PAD + 1 + size]
                store(rows, value)

    def stencil_half(h):
        def store(rows, value):
            ubuf[h, rows, :] = value
            ub16[rows, :] = value.astype(BF16)

        stencil(lambda c, r: zpad[h, c, r, :], lambda r: twice(shift_col[r, :]), store)

    def stencil_quarter():
        def store(rows, value):
            yq[rows, :] = value

        stencil(lambda c, r: zq[c, r, :], lambda r: shift_col[r, :], store)

    def prepare(h):
        coarse = coarse_half(1, h)
        tile = tile_of(n, 768, 16)

        @pl.loop(0, n // tile)
        def _(i):
            rows = pl.ds(pl.multiple_of(i * tile, tile), tile)
            ubuf[h, rows, :] = local[1, h, rows, :].astype(F32) + dot(basis_t[rows, :], coarse)

    def fold(value):
        return jnp.sum(value.reshape(value.shape[0] // 8, 8, LANES), axis=0)

    def inner_products(terms):
        tile = tile_of(n, 768, 16)

        def step(i, sums):
            rows = pl.ds(pl.multiple_of(i * tile, tile), tile)
            return tuple(s + fold(t) for s, t in zip(sums, terms(rows)))

        zero = jnp.zeros((8, LANES), F32)
        sums = lax.fori_loop(0, n // tile, step, (zero, zero, zero))
        rows = [jnp.sum(value, axis=0, keepdims=True) for value in sums]
        return jnp.concatenate(rows + [jnp.zeros((5, LANES), F32)], axis=0)

    def first_terms(rows):
        b = side(bv[my_half, rows, :]).astype(F32)
        u = side(ubuf[my_half, rows, :] - 4.0 * dot(place[rows, :], frecv[my_half]))
        uq[rows, :] = u
        return b * b, u * b, u * u

    def second_terms(h11, rows):
        b = side(bv[my_half, rows, :]).astype(F32)
        u = uq[rows, :]
        g = yq[rows, :] - 4.0 * dot(place[rows, :], frecv_q[...]) - h11 * u
        t = u - h11 * b
        return g * b, g * t, g * g

    def reduce_begin(it, partial):
        rb1[it, j] = partial
        mine = rb1.at[it, j]
        return [
            remote(mine, mine, at_j(k), rb1.at[it, lax.rem(j + nj - k, nj)]) for k in range(1, nj)
        ]

    def reduce_z(it, waits):
        wait_all(waits)
        rb2[it, z] = jnp.sum(rb1[it], axis=0)
        mine = rb2.at[it, z]
        return [
            remote(mine, mine, at_z(k), rb2.at[it, lax.rem(z + nz - k, nz)]) for k in range(1, nz)
        ]

    def reduce_end(it, waits):
        wait_all(waits)
        total = jnp.sum(rb2[it], axis=0)
        return total[0:1], total[1:2], total[2:3]

    def build_pads():
        for i in range(n // LANES):
            block = wide[:, i * LANES : (i + 1) * LANES]
            basis_t[pl.ds(i * LANES, LANES), :] = block.T.astype(BF16)
        for h in range(2):
            for comp in range(3):
                for start in (0, cells + PAD):
                    zpad[h, comp, pl.ds(start, PAD), :] = jnp.zeros((PAD, HALF), F32)
        for comp in range(3):
            for start in (0, cells + PAD):
                zq[comp, pl.ds(start, PAD), :] = jnp.zeros((PAD, LANES), F32)
        for i in range(n // LANES):
            row = jnp.broadcast_to(shift_ref[:, i * LANES : (i + 1) * LANES], (LANES, LANES))
            shift_col[pl.ds(i * LANES, LANES), :] = row.T

    lane = lax.broadcasted_iota(jnp.int32, (LANES, LANES), 1)
    line = lax.broadcasted_iota(jnp.int32, (LANES, LANES), 0)

    face_all = jnp.concatenate([face_ref[0:1, :], face_ref[1:2, :]], axis=1)

    def face_row(i):
        return jnp.broadcast_to(face_all[:, i * LANES : (i + 1) * LANES], (LANES, LANES))

    def build_pick():
        for i in range(faces // LANES):
            column = face_row(i).astype(F32).T.astype(jnp.int32)
            for k in range(n // LANES):
                hit = jnp.where(column == lane + k * LANES, 1.0, 0.0)
                pick[pl.ds(i * LANES, LANES), k * LANES : (k + 1) * LANES] = hit.astype(BF16)

    def build_place():
        for i in range(faces // LANES):
            slot = lane + i * LANES
            missing = ((slot < face) & (me_s == 0)) | ((slot >= face) & (me_s == subs - 1))
            row = jnp.where(missing, -1, face_row(i))
            for k in range(n // LANES):
                hit = jnp.where(row == line + k * LANES, 1.0, 0.0)
                place[pl.ds(k * LANES, LANES), i * LANES : (i + 1) * LANES] = hit.astype(BF16)

    def build_inv_place():
        for start, size in tiles:
            rows = pl.ds(start, size)
            width = tile_of(faces, 384, LANES)

            @pl.loop(0, faces // width)
            def _(i):
                cols = pl.ds(pl.multiple_of(i * width, width), width)
                inv_place[rows, cols] = dot(inv[rows, :], place[:, cols]).astype(BF16)

    def ready(i):
        if i == 0:
            loads[0].wait()
        loads[1 + i].wait()

    part_begin()
    first_product(0, ready)
    g00 = gather_begin(0, 0, True)
    loads[3].wait()
    first_product(1)
    coarse = coarse_begin(0)
    build_pads()
    g00_near = gather_begin(0, 0, False)
    build_pick()
    g00 = gather_forward(0, 0, g00)
    build_place()
    part_end()
    coarse = coarse_line(0, coarse)
    build_inv_place()
    wait_all(g00_near)
    g01 = gather_begin(0, 1, True)
    coarse = coarse_end(0, coarse)
    wait_all(g00)
    wait_all(coarse)
    assemble(0)
    g01_near = gather_begin(0, 1, False)
    f00 = faces_begin(zb, fsend.at[0], frecv.at[0])
    stencil_half(0)
    g01 = gather_forward(0, 1, g01)

    second_product(0)
    second_faces(0, f00)
    g10 = gather_begin(1, 0, True)
    wait_all(g01_near)
    wait_all(g01)
    assemble(1)
    f01 = faces_begin(zb, fsend.at[1], frecv.at[1])
    g10_near = gather_begin(1, 0, False)
    stencil_half(1)
    second_product(1)
    g10 = gather_forward(1, 0, g10)
    second_faces(1, f01)
    coarse = coarse_begin(1)

    prio_sem = used[0]
    used[0] += ny - 1
    own_part = pl.ds(base, nq)

    def prio_copy(k):
        target = lax.rem(me_y + k, ny)
        col = pl.multiple_of(lax.rem(target, 2) * LANES, LANES)
        return target, describe(
            prio_sem + k - 1,
            local.at[1, 1, own_part, pl.ds(col, LANES)],
            prio.at[own_part, :],
            at_y(k),
        )

    def prio_begin():
        for k in range(1, ny):
            target, cp = prio_copy(k)

            @pl.when(target // 2 == 1)
            def _(cp=cp):
                cp.start()

        @pl.when(my_half == 1)
        def _():
            prio[own_part, :] = side(local[1, 1, own_part, :].astype(F32)).astype(BF16)

    def prio_end():
        for k in range(1, ny):
            target, cp = prio_copy(k)

            @pl.when(target // 2 == 1)
            def _(cp=cp):
                cp.wait_send()

        @pl.when(my_half == 1)
        def _():
            for k in range(1, ny):
                source = lax.rem(me_y + ny - k, ny)
                slot = prio.at[pl.ds(pl.multiple_of(source * nq, nq), nq), :]
                describe(prio_sem + k - 1, slot, slot, at_y(k)).wait_recv()

    prio_begin()
    r0 = reduce_begin(0, inner_products(first_terms))
    coarse = coarse_line(1, coarse)
    g11 = gather_begin(1, 1, True)
    r0 = reduce_z(0, r0)
    g11_near = gather_begin(1, 1, False)
    coarse = coarse_end(1, coarse)
    prio_end()
    wait_all(g10_near)
    wait_all(g10)

    @pl.when(my_half == 0)
    def _():
        assemble_quarter(lambda rows: side(local[1, 0, rows, :].astype(F32)))

    @pl.when(my_half == 1)
    def _():
        assemble_quarter(lambda rows: prio[rows, :])

    f1 = faces_begin(zbq, fsend_q, frecv_q)
    g11 = gather_forward(1, 1, g11)
    bb, ub, uu = reduce_end(0, r0)
    stencil_quarter()
    beta2 = bb + 1e-12
    beta = jnp.sqrt(beta2)
    h11 = ub / beta2
    h21s = jnp.maximum((uu - h11 * (2.0 * ub - h11 * bb)) / beta2, 0.0) + 1e-12
    h21 = jnp.sqrt(h21s)
    wait_all(f1)
    r1 = reduce_begin(1, inner_products(functools.partial(second_terms, h11)))
    wait_all(coarse)
    prepare(0)
    r1 = reduce_z(1, r1)
    wait_all(g11_near)
    wait_all(g11)
    prepare(1)
    gb, gt, gg = reduce_end(1, r1)

    scale = 1.0 / (beta * h21)
    h12 = gb * scale / beta
    h22 = gt * scale * scale
    ww = gg * scale * scale
    ff_gap = 1e-12 / beta2
    ss_gap = 1e-12 / h21s
    fs = h11 * ff_gap / h21
    h32s = ww - h12 * h12 * (1.0 + ff_gap) - h22 * h22 * (1.0 + ss_gap) + 2.0 * h12 * h22 * fs
    h32 = jnp.sqrt(jnp.maximum(h32s, 0.0) + 1e-12)
    dist_one = jnp.sqrt(h11 * h11 + h21 * h21)
    cos_one = h11 / dist_one
    sin_one = h21 / dist_one
    r12 = cos_one * h12 + sin_one * h22
    t22 = cos_one * h22 - sin_one * h12
    dist_two = jnp.sqrt(t22 * t22 + h32 * h32)
    cos_two = t22 / dist_two
    sin_two = h32 / dist_two
    y2 = -cos_two * sin_one * beta / dist_two
    y1 = (cos_one * beta - r12 * y2) / dist_one
    weight_two = y2 * scale
    weight_one = y1 / beta - h11 * weight_two
    residual = jnp.abs(sin_one * sin_two)
    weights[me_y] = jnp.concatenate(
        [weight_one, weight_two, residual, jnp.zeros((5, LANES), F32)], axis=0
    )
    mine = weights.at[me_y]
    w1 = [
        remote(mine, mine, at_y(k), weights.at[lax.rem(me_y + ny - k, ny)]) for k in range(1, ny)
    ]

    def finish(h):
        def pair(i):
            return jnp.concatenate([weights[2 * h, i : i + 1], weights[2 * h + 1, i : i + 1]], axis=1)

        one_w, two_w, res = pair(0), pair(1), pair(2)
        res_ref[:, h * HALF : (h + 1) * HALF] = res
        tile = tile_of(cells, 256, 16)
        outs = []
        for comp in range(3):

            @pl.loop(0, cells // tile)
            def _(i, comp=comp):
                m0 = pl.multiple_of(i * tile, tile)
                rows = pl.ds(pl.multiple_of(comp * cells + m0, tile), tile)
                one = zpad[h, comp, pl.ds(m0 + PAD, tile), :]
                bv[h, rows, :] = (one * one_w + ubuf[h, rows, :] * two_w).astype(BF16)

            rows = pl.ds(comp * cells, cells)
            out = pltpu.make_async_copy(
                bv.at[h, rows, :],
                sol_hbm.at[rows, pl.ds(h * HALF, HALF)],
                lsem.at[5 + 3 * h + comp],
            )
            out.start()
            outs.append(out)
        return outs

    wait_all(w1)
    outs = finish(0)
    outs += finish(1)
    for cp in sent:
        cp.wait_send()
    for cp in outs:
        cp.wait()
    assert used[0] <= ssem.shape[0]


def count_copies(nz, nx, ny, rims):
    line, group = nz - 1, 2 * nx - 1
    coarse = 2 * (line + group + ny - 1)
    return 3 * (ny - 1) + coarse + 4 * 6 + 3 * rims + 2 * (group + line)


def per_device(nz, nx, right_sides, shift, inverses, basis, counts, face_rows, coarse_inverse):
    ny = lax.axis_size("crs")
    n, width = right_sides.shape[1:]
    nq = n // ny
    kmax = basis.shape[1]
    faces = 2 * face_rows.shape[2]
    cells = n // 3
    nj = 2 * nx
    subs = nz * nj
    ext = nq + kmax
    copies = count_copies(nz, nx, ny, 2 * (faces // 2 // tile_of(faces // 2, 288, 16)))
    any_spec = pl.BlockSpec(memory_space=pl.ANY)
    vmem = pl.BlockSpec(memory_space=pltpu.VMEM)
    out, residual = pl.pallas_call(
        functools.partial(kernel, (nz, nx, ny)),
        out_shape=(
            jax.ShapeDtypeStruct((n, width), BF16),
            jax.ShapeDtypeStruct((1, width), F32),
        ),
        in_specs=[
            any_spec,
            any_spec,
            any_spec,
            vmem,
            vmem,
            pl.BlockSpec(memory_space=pltpu.SMEM),
            vmem,
        ],
        out_specs=(any_spec, vmem),
        scratch_shapes=[
            pltpu.VMEM((2, n, HALF), BF16),
            pltpu.VMEM((ext, n), BF16),
            pltpu.VMEM((n, LANES), BF16),
            pltpu.VMEM((LANES, n), F32),
            pltpu.VMEM((n, LANES), F32),
            pltpu.VMEM((faces, n), BF16),
            pltpu.VMEM((n, faces), BF16),
            pltpu.VMEM((ext, faces), BF16),
            pltpu.VMEM((ext, HALF), F32),
            pltpu.VMEM((2, 2, n, HALF), BF16),
            pltpu.VMEM((n, LANES), BF16),
            pltpu.VMEM((2, 3, cells + 2 * PAD, HALF), F32),
            pltpu.VMEM((n, HALF), BF16),
            pltpu.VMEM((2, n, HALF), F32),
            pltpu.VMEM((n, HALF), BF16),
            pltpu.VMEM((2, faces, HALF), BF16),
            pltpu.VMEM((2, faces, HALF), BF16),
            pltpu.VMEM((3, cells + 2 * PAD, LANES), F32),
            pltpu.VMEM((n, LANES), BF16),
            pltpu.VMEM((n, LANES), F32),
            pltpu.VMEM((n, LANES), F32),
            pltpu.VMEM((faces, LANES), BF16),
            pltpu.VMEM((faces, LANES), BF16),
            pltpu.VMEM((nj * kmax, subs * kmax), BF16),
            pltpu.VMEM((subs * kmax, nz * kmax), BF16),
            pltpu.VMEM((nj * kmax, nz * kmax), BF16),
            pltpu.VMEM((2, 2, kmax, HALF), F32),
            pltpu.VMEM((2, nz, kmax, LANES), BF16),
            pltpu.VMEM((2, nj, kmax, LANES), F32),
            pltpu.VMEM((2, nj, kmax, LANES), F32),
            pltpu.VMEM((2, ny, kmax, LANES), BF16),
            pltpu.VMEM((2, nj, 8, LANES), F32),
            pltpu.VMEM((2, nz, 8, LANES), F32),
            pltpu.VMEM((ny, 8, LANES), F32),
            pltpu.SemaphoreType.DMA((copies,)),
            pltpu.SemaphoreType.DMA((copies,)),
            pltpu.SemaphoreType.DMA((11,)),
        ],
        compiler_params=pltpu.CompilerParams(
            collective_id=0, has_side_effects=True, vmem_limit_bytes=60 * 1024 * 1024
        ),
    )(
        right_sides[0],
        inverses[0],
        coarse_inverse,
        shift,
        basis[0],
        counts,
        face_rows[0],
    )
    return out[None], residual.reshape(width)


def solution(mesh):
    subs = mesh.shape["sub"]
    nz = 8 if subs == 64 else subs // 2
    nx = subs // (2 * nz)
    return jax.shard_map(
        functools.partial(per_device, nz, nx),
        mesh=mesh,
        in_specs=(
            P("sub", None, None),
            P("sub", None),
            P("sub", "crs", None),
            P("sub", None, None),
            P("sub"),
            P("sub", None, None),
            P("crs", None),
        ),
        out_specs=(P("sub", None, None), P()),
        check_vma=False,
    )
```

time: 1150 us -> 92.2 us (0.08)
  blocking collectives: 784 us -> 0 us
  waiting for transfers between devices: 181 us -> 0 us
  other arithmetic: 97.9 us -> 0 us
  Pallas kernels: 0 us -> 86.9 us
  matrix products: 26.6 us -> 0 us
  local copies, waits for them, and re-layouts: 29.9 us -> 3.81 us
  between operations: 14.7 us -> 1.29 us
  starting transfers between devices: 11.5 us -> 0 us
    psum x8 -> x0, blocking collectives: 784 us -> none  [the longest x3 380 us: norm_of(): lax.psum(jnp.sum(vector_in * vector_in, axis=0), 'sub') + 1e-12]
    all_gather x4 -> x0, waiting for transfers between devices: 181 us -> none  [the longest x2 142 us: precondition(): lax.all_gather(coefficients, 'sub', axis=0, tiled=True)]
    pallas_call x0 -> x1, Pallas kernels: none -> 86.9 us  [per_device(): pl.pallas_call(functools.partial(kernel, (nz, nx, ny)), out_shape=(jax.Sh...]
    scatter-add x4 -> x0, other arithmetic: 47.4 us -> none  [the longest x2 23.8 us: apply_operator(): applied = applied.at[face_rows[0]].add(-4.0 * from_below)]
    reduce_sum x8 -> x0, other arithmetic: 30.7 us -> none  [the longest x3 11.7 us: inner_sum(): return lax.psum(jnp.sum(first_vec * second_vec, axis=0), 'sub')]
    dot_general x8 -> x0, matrix products: 26.6 us -> none  [the longest x2 9.47 us: precondition(): lax.dot_general(masked_basis, coarse_values, (((0,), (0,)), ((), ())), pr...]
    gather x2 -> x0, local copies, waits for them, and re-layouts: 13.8 us -> none  [neighbour_rims(): jnp.take(vector_in, face_rows.reshape(-1), axis=0)]
    slice x4 -> x0, local copies, waits for them, and re-layouts: 13.5 us -> none  [the longest x2 10.2 us: apply_operator(): below_cells = jnp.concatenate([zero_column, component_grid[:, :-1]], axis=1)]
  transfers between devices with their start and end apart: 8 -> 0, of which waited for: 4 -> 0; matrix products, arithmetic and copies ran while one was open for 5% -> 0% of each run, Pallas kernels for 0% -> 0%
where the time goes in v2:
time: 92.2 us; the launch traced here: 92 us
  Pallas kernels  86.9 us (94%)
  local copies, waits for them, and re-layouts  3.81 us (4%)
  between operations  1.29 us (1%)
    pallas_call x1, Pallas kernels, per_device(): pl.pallas_call(functools.partial(kernel, (nz, nx, ny)), out_shape=(jax.Sh...  86.9 us
    unnamed x4, local copies, waits for them, and re-layouts  3.81 us

profile of v2, /device:TPU:1, one launch (start us, length us, event | category | flops | bytes accessed | tf_op | source)
XLA Modules:
  0.0 92.0 jit_solution(9568273696380049106)
XLA Ops:
  1.3 86.9 %shard_map.86 = (bf16[2304,512]{1,0:T(8,128)(2,1)}, f32[1,512]{1,0:T(1,128)}) custom-call(bf16[2304,512]{1,0:T(8,128)(2,1)} %bitcast.7, bf16[576,2304]{1,0:T(8,128)(2,1)} %bitcast.6, bf16[512,2048]{1,0:T(8,128)(2,1)} %cinv_hbm.1, f32[1,2304]{1,0:T(1,128)} %shift_ref.1, bf16[32,2304]{1,0:T(8,128)(2,1)} %bitcast.9, s32[1]{0:T(128)S(6)} %copy.11.count_ref, ...), custom_call_target="tpu_custom_call" | custom-call | tf_op jit(solution)/shard_map/pallas_call | solution.py:693
  88.2 0.0 copy-start
  88.2 3.2 %copy.12 = bf16[1,2304,512]{2,1,0:T(8,128)(2,1)} copy(bf16[1,2304,512]{2,1,0:T(8,128)(2,1)} %bitcast.8) | data formatting | bytes 4718592
  91.4 0.0 copy-done
  91.4 0.6 copy.13
Async XLA Ops:
  88.2 3.2 %copy-start = (f32[1,512]{1,0:T(1,128)S(1)}, f32[1,512]{1,0:T(1,128)}, u32[]{:S(2)}) copy-start(f32[1,512]{1,0:T(1,128)} %get-tuple-element.5) | copy-start | bytes 6148

commit v3 on v2

--- a/solution.py
+++ b/solution.py
@@ -65,8 +65,6 @@
     uq,
     fsend_q,
     frecv_q,
-    crows,
-    select,
     cpart,
     coef,
     cg,
@@ -159,82 +157,57 @@
     for device in partners:
         pl.semaphore_signal(barrier, inc=1, device_id=device, device_id_type=MESH)
 
-    panel = cinv_hbm.shape[0]
-    line_rows = nj * kmax
-    owner = z * line_rows // panel
-    offset = pl.multiple_of(lax.rem(z * line_rows, panel), line_rows)
-    own_rows = pltpu.make_async_copy(cinv_hbm.at[pl.ds(offset, line_rows), :], crows, lsem.at[4])
-
-    @pl.when(me_y == owner)
-    def _():
-        own_rows.start()
-
     keep = lax.broadcasted_iota(jnp.int32, (kmax, n), 0) < count_ref[0]
     masked = jnp.where(keep, basis_ref[...].astype(F32), 0.0)
     inv[pl.ds(nq, kmax), :] = masked.astype(BF16)
     wide[...] = jnp.zeros_like(wide)
     wide[pl.ds(0, kmax), :] = masked
 
-    @pl.when(me_y == owner)
-    def _():
-        at = lax.broadcasted_iota(jnp.int32, select.shape, 0)
-        col = lax.broadcasted_iota(jnp.int32, select.shape, 1)
-        wanted = (col // kmax) * line_rows + j * kmax + lax.rem(col, kmax)
-        select[...] = jnp.where(at == wanted, 1.0, 0.0).astype(BF16)
-        own_rows.wait()
-        cpart[...] = dot(crows[...], select[...]).astype(BF16)
-
     pl.semaphore_wait(barrier, len(partners))
 
+    mine_z = cinv_hbm.shape[0]
     part_sem = used[0]
     used[0] += ny - 1
-
-    def part_copy(k):
-        return pltpu.make_async_remote_copy(
-            src_ref=cpart,
-            dst_ref=cpart,
-            send_sem=ssem.at[part_sem + k - 1],
-            recv_sem=rsem.at[part_sem],
-            device_id=at_y(k),
-            device_id_type=MESH,
-        )
+    wanted = cinv_hbm.at[:, j, :, pl.ds(pl.multiple_of(z * nj * kmax, nj * kmax), nj * kmax)]
+
+    def part_slot(k):
+        return cpart.at[pl.ds(lax.rem(me_y + k, ny) * mine_z, mine_z)]
+
+    own_part_copy = pltpu.make_async_copy(wanted, part_slot(0), lsem.at[4])
+    own_part_copy.start()
 
     def part_begin():
-        @pl.when(me_y == owner)
-        def _():
-            for k in range(1, ny):
-                part_copy(k).start()
+        for k in range(1, ny):
+            describe(part_sem + k - 1, wanted, part_slot(0), at_y(k)).start()
 
     def part_end():
-        @pl.when(me_y == owner)
-        def _():
-            for k in range(1, ny):
-                part_copy(k).wait_send()
-
-        @pl.when(me_y != owner)
-        def _():
-            part_copy(1).wait_recv()
+        own_part_copy.wait()
+        for k in range(1, ny):
+            describe(part_sem + k - 1, wanted, part_slot(0), at_y(k)).wait_send()
+            slot = part_slot(ny - k)
+            describe(part_sem + k - 1, slot, slot, at_y(k)).wait_recv()
 
     def coarse_begin(it):
-        cg[it, z] = side(coef[it, my_half]).astype(BF16)
-        mine = cg.at[it, z]
+        cg[it, j] = side(coef[it, my_half]).astype(BF16)
+        mine = cg.at[it, j]
         return [
-            remote(mine, mine, at_z(k), cg.at[it, lax.rem(z + nz - k, nz)]) for k in range(1, nz)
+            remote(mine, mine, at_j(k), cg.at[it, lax.rem(j + nj - k, nj)]) for k in range(1, nj)
         ]
 
     def coarse_line(it, waits):
         wait_all(waits)
-        partial = dot(cpart[...], cg[it].reshape(nz * kmax, LANES))
-        cpsend[it] = partial.reshape(nj, kmax, LANES)
-        cprecv[it, j] = cpsend[it, j]
+        rows = cpart[...].reshape(nz * kmax, nj * kmax)
+        partial = dot(rows, cg[it].reshape(nj * kmax, LANES))
+        cpsend[it] = partial.reshape(nz, kmax, LANES)
+        cprecv[it, z] = cpsend[it, z]
         return [
             remote(
-                cpsend.at[it, lax.rem(j + k, nj)],
-                cprecv.at[it, j],
-                at_j(k),
-                cprecv.at[it, lax.rem(j + nj - k, nj)],
+                cpsend.at[it, lax.rem(z + k, nz)],
+                cprecv.at[it, z],
+                at_z(k),
+                cprecv.at[it, lax.rem(z + nz - k, nz)],
             )
-            for k in range(1, nj)
+            for k in range(1, nz)
         ]
 
     def coarse_end(it, waits):
@@ -730,13 +703,11 @@
             pltpu.VMEM((n, LANES), F32),
             pltpu.VMEM((faces, LANES), BF16),
             pltpu.VMEM((faces, LANES), BF16),
-            pltpu.VMEM((nj * kmax, subs * kmax), BF16),
-            pltpu.VMEM((subs * kmax, nz * kmax), BF16),
-            pltpu.VMEM((nj * kmax, nz * kmax), BF16),
+            pltpu.VMEM((nz, kmax, nj * kmax), BF16),
             pltpu.VMEM((2, 2, kmax, HALF), F32),
-            pltpu.VMEM((2, nz, kmax, LANES), BF16),
-            pltpu.VMEM((2, nj, kmax, LANES), F32),
-            pltpu.VMEM((2, nj, kmax, LANES), F32),
+            pltpu.VMEM((2, nj, kmax, LANES), BF16),
+            pltpu.VMEM((2, nz, kmax, LANES), F32),
+            pltpu.VMEM((2, nz, kmax, LANES), F32),
             pltpu.VMEM((2, ny, kmax, LANES), BF16),
             pltpu.VMEM((2, nj, 8, LANES), F32),
             pltpu.VMEM((2, nz, 8, LANES), F32),
@@ -751,7 +722,7 @@
     )(
         right_sides[0],
         inverses[0],
-        coarse_inverse,
+        coarse_inverse.reshape(-1, nj, kmax, subs * kmax),
         shift,
         basis[0],
         counts,

time: 92.2 us -> 89 us (0.965)
  Pallas kernels: 86.9 us -> 83.8 us
    pallas_call x1, Pallas kernels: 86.9 us -> 83.8 us  [per_device(): pl.pallas_call(functools.partial(kernel, (nz, nx, ny)), out_shape=(jax.Sh...]
where the time goes in v3:
time: 89 us; the launch traced here: 88.9 us
  Pallas kernels  83.8 us (94%)
  local copies, waits for them, and re-layouts  3.81 us (4%)
  between operations  1.29 us (1%)
    pallas_call x1, Pallas kernels, per_device(): pl.pallas_call(functools.partial(kernel, (nz, nx, ny)), out_shape=(jax.Sh...  83.8 us
    unnamed x4, local copies, waits for them, and re-layouts  3.81 us

profile of v3, /device:TPU:1, one launch (start us, length us, event | category | flops | bytes accessed | tf_op | source)
XLA Modules:
  0.0 88.9 jit_solution(13855515672516456044)
XLA Ops:
  1.3 83.8 %shard_map.86 = (bf16[2304,512]{1,0:T(8,128)(2,1)}, f32[1,512]{1,0:T(1,128)}) custom-call(bf16[2304,512]{1,0:T(8,128)(2,1)} %bitcast.8, bf16[576,2304]{1,0:T(8,128)(2,1)} %bitcast.7, bf16[2,8,32,2048]{3,2,1,0:T(8,128)(2,1)} %bitcast.10, f32[1,2304]{1,0:T(1,128)} %shift_ref.1, bf16[32,2304]{1,0:T(8,128)(2,1)} %bitcast.11, s32[1]{0:T(128)S(6)} %copy.11.count_ref, ...), custom_call_target="tpu_custom_call" | custom-call | tf_op jit(solution)/shard_map/pallas_call | solution.py:666
  85.1 0.0 copy-start
  85.1 3.2 %copy.12 = bf16[1,2304,512]{2,1,0:T(8,128)(2,1)} copy(bf16[1,2304,512]{2,1,0:T(8,128)(2,1)} %bitcast.9) | data formatting | bytes 4718592
  88.3 0.0 copy-done
  88.3 0.6 copy.13
Async XLA Ops:
  85.1 3.2 %copy-start = (f32[1,512]{1,0:T(1,128)S(1)}, f32[1,512]{1,0:T(1,128)}, u32[]{:S(2)}) copy-start(f32[1,512]{1,0:T(1,128)} %get-tuple-element.5) | copy-start | bytes 6148

commit v4 on v3

--- a/solution.py
+++ b/solution.py
@@ -308,7 +308,7 @@
     lower, upper = pl.ds(0, face), pl.ds(face, face)
 
     def faces_begin(field, out, into):
-        tile = tile_of(face, 288, 16)
+        tile = tile_of(face, 192, 16)
         waits = []
         for start in range(0, face, tile):
             for first, other, device in ((face, 0, above), (0, face, below)):
@@ -660,7 +660,7 @@
     nj = 2 * nx
     subs = nz * nj
     ext = nq + kmax
-    copies = count_copies(nz, nx, ny, 2 * (faces // 2 // tile_of(faces // 2, 288, 16)))
+    copies = count_copies(nz, nx, ny, 2 * (faces // 2 // tile_of(faces // 2, 192, 16)))
     any_spec = pl.BlockSpec(memory_space=pl.ANY)
     vmem = pl.BlockSpec(memory_space=pltpu.VMEM)
     out, residual = pl.pallas_call(

time: 89 us -> 88 us (0.989)
  Pallas kernels: 83.8 us -> 82.8 us
    pallas_call x1, Pallas kernels: 83.8 us -> 82.8 us  [per_device(): pl.pallas_call(functools.partial(kernel, (nz, nx, ny)), out_shape=(jax.Sh...]
where the time goes in v4:
time: 88 us; the launch traced here: 87.9 us
  Pallas kernels  82.8 us (94%)
  local copies, waits for them, and re-layouts  3.81 us (4%)
  between operations  1.29 us (1%)
    pallas_call x1, Pallas kernels, per_device(): pl.pallas_call(functools.partial(kernel, (nz, nx, ny)), out_shape=(jax.Sh...  82.8 us
    unnamed x4, local copies, waits for them, and re-layouts  3.81 us

profile of v4, /device:TPU:1, one launch (start us, length us, event | category | flops | bytes accessed | tf_op | source)
XLA Modules:
  0.0 87.9 jit_solution(9865355334972875604)
XLA Ops:
  1.3 82.8 %shard_map.86 = (bf16[2304,512]{1,0:T(8,128)(2,1)}, f32[1,512]{1,0:T(1,128)}) custom-call(bf16[2304,512]{1,0:T(8,128)(2,1)} %bitcast.8, bf16[576,2304]{1,0:T(8,128)(2,1)} %bitcast.7, bf16[2,8,32,2048]{3,2,1,0:T(8,128)(2,1)} %bitcast.10, f32[1,2304]{1,0:T(1,128)} %shift_ref.1, bf16[32,2304]{1,0:T(8,128)(2,1)} %bitcast.11, s32[1]{0:T(128)S(6)} %copy.11.count_ref, ...), custom_call_target="tpu_custom_call" | custom-call | tf_op jit(solution)/shard_map/pallas_call | solution.py:666
  84.1 0.0 copy-start
  84.1 3.2 %copy.12 = bf16[1,2304,512]{2,1,0:T(8,128)(2,1)} copy(bf16[1,2304,512]{2,1,0:T(8,128)(2,1)} %bitcast.9) | data formatting | bytes 4718592
  87.3 0.0 copy-done
  87.3 0.6 copy.13
Async XLA Ops:
  84.1 3.2 %copy-start = (f32[1,512]{1,0:T(1,128)S(1)}, f32[1,512]{1,0:T(1,128)}, u32[]{:S(2)}) copy-start(f32[1,512]{1,0:T(1,128)} %get-tuple-element.5) | copy-start | bytes 6148
